TPU v7x, 512 devices: a whole 4x4x16 slice. The times are simulated.
512 devices in a mesh: grp: 32 (over y, x, core), seq: 16 (over z).
Axes of the slice: x: 4, y: 4, z: 16, core: 2. Of those that a mesh axis runs over, the one named last changes fastest.
Arguments:
- q_space: bfloat16 [512, 256, 576], P(('grp', 'seq')), may hold values from -96 to 96
- k_space: bfloat16 [512, 256, 576], P(('grp', 'seq')), may hold values from -96 to 96
- v_space: bfloat16 [512, 256, 576], P(('grp', 'seq')), may hold values from -6 to 6
- cot_space: bfloat16 [512, 256, 576], P(('grp', 'seq')), may hold values from -6 to 6
- q_time: bfloat16 [512, 256, 576], P(('grp', 'seq')), may hold values from -96 to 96
- k_time: bfloat16 [512, 256, 576], P(('grp', 'seq')), may hold values from -96 to 96
- v_time: bfloat16 [512, 256, 576], P(('grp', 'seq')), may hold values from -6 to 6
- cot_time: bfloat16 [512, 256, 576], P(('grp', 'seq')), may hold values from -6 to 6
- clip_len: int32 [64], replicated, may hold values from 1 to 16, 512 in all
Outputs:
- grad_q_space: bfloat16 [512, 256, 576], P(('grp', 'seq'))
- grad_k_space: bfloat16 [512, 256, 576], P(('grp', 'seq'))
- grad_v_space: bfloat16 [512, 256, 576], P(('grp', 'seq'))
- grad_q_time: bfloat16 [512, 256, 576], P(('grp', 'seq'))
- grad_k_time: bfloat16 [512, 256, 576], P(('grp', 'seq'))
- grad_v_time: bfloat16 [512, 256, 576], P(('grp', 'seq'))
Inputs may be any that keep to these rules, and one draw needn't show every extreme that they name: `clip_len`: the 64 frame counts sum to 512; some clip has exactly 16 frames.
All inputs are finite; a program needn't handle non-finite values.
Results may differ from a plain program's by a relative error of at most 0.013.
Values may be sent and summed in bfloat16 or wider, within the bound.
A program may use at most 64 MiB of HBM per device.

v0:
```python
import functools
import math

import jax
import jax.numpy as jnp
from jax import lax
from jax.experimental import pallas as pl
from jax.experimental.pallas import tpu as pltpu
from jax.sharding import PartitionSpec as P

HEADS = 8
HDIM = 72
LANES = 128
SCALE = 1.0 / math.sqrt(HDIM)
MASKED = -1e30
MESH = pl.DeviceIdType.MESH
BF = jnp.bfloat16
F32 = jnp.float32


def space_head(h, qs, ks, vs, cs, gq, gk, gv):
    q, k, v, c = qs[h], ks[h], vs[h], cs[h]
    first = (((0,), (0,)), ((), ()))
    last = (((1,), (1,)), ((), ()))
    plain = (((1,), (0,)), ((), ()))
    scores = lax.dot_general(k, q, first, preferred_element_type=F32) * SCALE
    peak = jnp.max(scores, axis=0, keepdims=True)
    grown = jnp.exp(scores - peak)
    weights = grown * (1.0 / jnp.sum(grown, axis=0, keepdims=True))
    low = weights.astype(BF)
    dweights = lax.dot_general(v, c, first, preferred_element_type=F32)
    dot = jnp.sum(low.astype(F32) * dweights, axis=0, keepdims=True)
    dscores = (weights * (dweights - dot)).astype(BF)
    gq[h] = (lax.dot_general(k, dscores, plain, preferred_element_type=F32) * SCALE).astype(BF)
    gk[h] = (lax.dot_general(q, dscores, last, preferred_element_type=F32) * SCALE).astype(BF)
    gv[h] = lax.dot_general(c, low, last, preferred_element_type=F32).astype(BF)


def kernel(
    nz, ng,
    qs, ks, vs, cs, qt, kt, vt, ct, labels, side,
    gqs, gks, gvs, gqt, gkt, gvt,
    s1, s2, s3, r1, r2, r3, o1, o2, t1, t2,
    fq, fk, fv, fg, fw, fl, fd,
    in_send, in_recv, hop_send, hop_recv, out_send, out_recv, self_sem,
):
    g = lax.axis_index("grp")
    z = lax.axis_index("seq")
    before = lax.rem(g + ng - 1, ng)
    after = lax.rem(g + 1, ng)

    def partner(d):
        return lax.rem(z + d, nz)

    barrier = pltpu.get_barrier_semaphore()
    for d in range(1, nz):
        pl.semaphore_signal(barrier, inc=1, device_id=(g, partner(d)), device_id_type=MESH)
    pl.semaphore_signal(barrier, inc=1, device_id=(before, z), device_id_type=MESH)
    pl.semaphore_signal(barrier, inc=1, device_id=(after, z), device_id_type=MESH)

    halves = [slice(0, LANES), slice(LANES, 2 * LANES)]
    for h in range(HEADS):
        for half in range(2):
            p = 2 * h + half
            s1[p, 0:HDIM, :] = qt[h, :, halves[half]]
            s1[p, HDIM : 2 * HDIM, :] = kt[h, :, halves[half]]
    pl.semaphore_wait(barrier, nz - 1 + 2)

    order = []
    for d in range(1, nz // 2):
        order += [d, nz - d]
    order.append(nz // 2)

    def send(stage, src, dst, sems_out, sems_in, d):
        return pltpu.make_async_remote_copy(
            src_ref=src.at[partner(d)], dst_ref=dst.at[z],
            send_sem=sems_out.at[stage, d], recv_sem=sems_in.at[stage, d],
            device_id=(g, partner(d)), device_id_type=MESH,
        )

    def own(src, dst, i):
        return pltpu.make_async_copy(src.at[z], dst.at[z], self_sem.at[i])

    def hop(stage, ref):
        return [
            pltpu.make_async_remote_copy(
                src_ref=ref.at[1], dst_ref=ref.at[0], send_sem=hop_send.at[stage, 0],
                recv_sem=hop_recv.at[stage, 0], device_id=(after, z), device_id_type=MESH,
            ),
            pltpu.make_async_remote_copy(
                src_ref=ref.at[1], dst_ref=ref.at[2], send_sem=hop_send.at[stage, 1],
                recv_sem=hop_recv.at[stage, 1], device_id=(before, z), device_id_type=MESH,
            ),
        ]

    firsts = [send(0, s1, r1.at[1], in_send, in_recv, d) for d in order]
    firsts.append(own(s1, r1.at[1], 0))
    for c in firsts:
        c.start()
    for h in range(HEADS):
        for half in range(2):
            p = 2 * h + half
            s2[p, 0:HDIM, :] = ct[h, :, halves[half]]
            s2[p, HDIM:, :] = vt[h, 0:8, halves[half]]
            s3[p] = vt[h, 8:, halves[half]]

    @pl.loop(0, HEADS)
    def _(h):
        space_head(h, qs, ks, vs, cs, gqs, gks, gvs)

    seconds = [send(1, s2, r2.at[1], in_send, in_recv, d) for d in order]
    seconds.append(own(s2, r2.at[1], 1))
    for c in seconds:
        c.start()
    for c in firsts:
        c.wait()
    hop1 = hop(0, r1)
    for c in hop1:
        c.start()
    thirds = [send(2, s3, r3.at[1], in_send, in_recv, d) for d in order]
    thirds.append(own(s3, r3.at[1], 2))
    for c in thirds:
        c.start()

    def lay(n, target, row, ref, low, high, at):
        count = high - low
        mine = ref[1, row, low:high, :].astype(F32)
        if n == 1:
            target[1, row, at : at + count, :] = mine
        else:
            other = ref[n, row, low:high, :].astype(F32)
            keep = side[n, row] > 0.5
            target[n, row, at : at + count, :] = jnp.where(keep[0:1, :], mine, other)

    def scores_of(n):
        label = labels[n]
        @pl.loop(0, nz)
        def _(i):
            s = jnp.sum(fq[n, i][None] * fk[n], axis=1) * SCALE
            same = label == labels[n, pl.ds(i, 1), :]
            s = jnp.where(same, s, MASKED)
            e = jnp.where(same, jnp.exp(s - jnp.max(s, axis=0, keepdims=True)), 0.0)
            w = e * (1.0 / jnp.sum(e, axis=0, keepdims=True))
            low = w.astype(BF).astype(F32)
            fw[n, i] = w
            fl[n, i] = jnp.broadcast_to(low[:, None, :], (nz, 8, LANES))

    def sum_over(rows, coef):
        acc = jnp.zeros((HDIM // 8, 8, LANES), F32)
        for m in range(nz):
            acc = acc + rows(m).reshape(HDIM // 8, 8, LANES) * coef(m)[None]
        return acc.reshape(HDIM, LANES)

    @pl.loop(0, nz)
    def _(i):
        lay(1, fq, i, r1, 0, HDIM, 0)
        lay(1, fk, i, r1, HDIM, 2 * HDIM, 0)

    scores_of(1)
    for c in hop1:
        c.wait()

    @pl.loop(0, nz)
    def _(i):
        for n in (0, 2):
            lay(n, fq, i, r1, 0, HDIM, 0)
            lay(n, fk, i, r1, HDIM, 2 * HDIM, 0)

    scores_of(0)
    scores_of(2)

    for c in seconds:
        c.wait()
    hop2 = hop(1, r2)
    for c in hop2:
        c.start()
    for c in hop2:
        c.wait()

    @pl.loop(0, nz)
    def _(i):
        for n in range(3):
            lay(n, fg, i, r2, 0, HDIM, 0)

    def pick(j, a, b, c):
        left = side[0, j, 0:1, :] > 0.5
        right = side[2, j, 0:1, :] > 0.5
        return jnp.where(left, a, jnp.where(right, c, b))

    @pl.loop(0, nz)
    def _(j):
        parts = [sum_over(lambda i: fg[n, i], lambda i: fl[n, i, j]) for n in range(3)]
        o1[j, 0:HDIM, :] = pick(j, *parts).astype(BF)
        o1[j, HDIM:, :] = jnp.zeros((8, LANES), BF)

    for c in thirds:
        c.wait()
    hop3 = hop(2, r3)
    for c in hop3:
        c.start()
    vouts = [send(0, o1, t1, out_send, out_recv, d) for d in order]
    vouts.append(own(o1, t1, 3))
    for c in vouts:
        c.start()
    for c in hop3:
        c.wait()

    @pl.loop(0, nz)
    def _(i):
        for n in range(3):
            lay(n, fv, i, r2, HDIM, HDIM + 8, 0)
            lay(n, fv, i, r3, 0, HDIM - 8, 8)

    @pl.loop(0, nz)
    def _(i):
        for n in range(3):
            dw = jnp.sum(fg[n, i][None] * fv[n], axis=1)
            w = fw[n, i]
            low = w.astype(BF).astype(F32)
            dot = jnp.sum(low * dw, axis=0, keepdims=True)
            ds = (w * (dw - dot)).astype(BF).astype(F32)
            fd[n, i] = jnp.broadcast_to(ds[:, None, :], (nz, 8, LANES))

    @pl.loop(0, nz)
    def _(i):
        parts = [sum_over(lambda j: fk[n, j], lambda j: fd[n, i, j]) for n in range(3)]
        o2[i, 0:HDIM, :] = (pick(i, *parts) * SCALE).astype(BF)
        parts = [sum_over(lambda j: fq[n, j], lambda j: fd[n, j, i]) for n in range(3)]
        o2[i, HDIM:, :] = (pick(i, *parts) * SCALE).astype(BF)

    qkouts = [send(1, o2, t2, out_send, out_recv, d) for d in order]
    qkouts.append(own(o2, t2, 4))
    for c in qkouts:
        c.start()
    for c in vouts:
        c.wait()
    for h in range(HEADS):
        for half in range(2):
            gvt[h, :, halves[half]] = t1[2 * h + half, 0:HDIM, :]
    for c in qkouts:
        c.wait()
    for h in range(HEADS):
        for half in range(2):
            gqt[h, :, halves[half]] = t2[2 * h + half, 0:HDIM, :]
            gkt[h, :, halves[half]] = t2[2 * h + half, HDIM:, :]


def clip_sides(clip_len, nz, ng):
    g = lax.axis_index("grp")
    first = g * nz
    ids = first - nz + jnp.arange(3 * nz, dtype=jnp.int32)
    ends = jnp.cumsum(clip_len)
    label = jnp.sum((ends[None, :] <= ids[:, None]).astype(jnp.int32), axis=1)
    label = jnp.where((ids >= 0) & (ids < nz * ng), label, -1)
    own = label[nz : 2 * nz]
    left = own == label[nz - 1]
    right = own == label[2 * nz]
    lab = jnp.stack(
        [jnp.where(left, own, label[:nz]), own, jnp.where(right, own, label[2 * nz :])]
    )
    side = jnp.stack([left, jnp.ones_like(left), right])
    lab = jnp.broadcast_to(lab.astype(F32)[:, :, None], (3, nz, LANES))
    side = jnp.broadcast_to(side.astype(F32)[:, :, None, None], (3, nz, 8, LANES))
    return lab, side


def solution(mesh):
    nz, ng = mesh.shape["seq"], mesh.shape["grp"]

    def shards(*args):
        clip_len = args[8]
        _, tokens, channels = args[0].shape
        flat = [jnp.swapaxes(a[0], 0, 1).reshape(HEADS, HDIM, tokens) for a in args[:8]]
        lab, side = clip_sides(clip_len, nz, ng)
        vmem = pl.BlockSpec(memory_space=pltpu.VMEM)
        dma = pltpu.SemaphoreType.DMA
        res = pl.pallas_call(
            functools.partial(kernel, nz, ng),
            out_shape=[jax.ShapeDtypeStruct((HEADS, HDIM, tokens), BF)] * 6,
            in_specs=[vmem] * 10,
            out_specs=[vmem] * 6,
            scratch_shapes=[
                pltpu.VMEM((nz, 2 * HDIM, LANES), BF),
                pltpu.VMEM((nz, HDIM + 8, LANES), BF),
                pltpu.VMEM((nz, HDIM - 8, LANES), BF),
                pltpu.VMEM((3, nz, 2 * HDIM, LANES), BF),
                pltpu.VMEM((3, nz, HDIM + 8, LANES), BF),
                pltpu.VMEM((3, nz, HDIM - 8, LANES), BF),
                pltpu.VMEM((nz, HDIM + 8, LANES), BF),
                pltpu.VMEM((nz, 2 * HDIM, LANES), BF),
                pltpu.VMEM((nz, HDIM + 8, LANES), BF),
                pltpu.VMEM((nz, 2 * HDIM, LANES), BF),
                pltpu.VMEM((3, nz, HDIM, LANES), F32),
                pltpu.VMEM((3, nz, HDIM, LANES), F32),
                pltpu.VMEM((3, nz, HDIM, LANES), F32),
                pltpu.VMEM((3, nz, HDIM, LANES), F32),
                pltpu.VMEM((3, nz, nz, LANES), F32),
                pltpu.VMEM((3, nz, nz, 8, LANES), F32),
                pltpu.VMEM((3, nz, nz, 8, LANES), F32),
                dma((3, nz)), dma((3, nz)), dma((3, 2)), dma((3, 2)), dma((2, nz)), dma((2, nz)),
                dma((5,)),
            ],
            compiler_params=pltpu.CompilerParams(
                collective_id=0, has_side_effects=True, vmem_limit_bytes=48 << 20
            ),
        )(*flat, lab, side)
        return tuple(jnp.swapaxes(r.reshape(channels, tokens), 0, 1)[None] for r in res)

    cut = P(("grp", "seq"), None, None)
    return jax.shard_map(
        shards, mesh=mesh, in_specs=(cut,) * 8 + (P(),), out_specs=(cut,) * 6, check_vma=False
    )
```

profile of v0, /device:TPU:7, one launch (start us, length us, event | category | flops | bytes accessed | tf_op | source)
XLA Modules:
  0.0 135.8 jit_solution(12254774344779971347)
XLA Ops:
  0.6 0.0 copy-start
  0.7 0.1 pad.1.clone
  0.7 0.7 copy.17
  1.5 0.1 reduce-window.8
  1.6 0.1 reduce
  1.7 0.2 convert_reduce_fusion
  1.9 0.6 fusion.2
  2.5 1.4 %compare_bitcast_fusion.1 = (pred[1,16]{1,0:T(4,128)(4,1)S(1)}, pred[1,16]{1,0:T(4,128)(4,1)S(1)}) fusion(s32[]{:T(128)} %bitcast.25, s32[48]{0:T(128)S(1)} %and_select_fusion, s32[]{:T(128)} %bitcast.28), kind=kLoop, calls=%fused_computation.3 | loop fusion | flops 32 | bytes 104 | tf_op jit(solution)/shard_map/stack | solution.py:261
  3.8 1.4 %fusion = (s32[1,16]{1,0:T(1,128)S(1)}, s32[1,16]{1,0:T(1,128)S(1)}, s32[1,16]{1,0:T(1,128)S(1)}) fusion(s32[48]{0:T(128)S(1)} %and_select_fusion, s32[]{:T(128)} %bitcast.25, s32[]{:T(128)} %bitcast.28), kind=kLoop, calls=%fused_computation.8 | loop fusion | flops 64 | bytes 392 | tf_op jit(solution)/shard_map/stack | solution.py:258
  5.2 0.1 add_convert_fusion.1
  5.3 0.1 broadcast_in_dim.37.labels
  5.4 0.1 broadcast_in_dim.38.side
  5.5 0.0 copy-done
  5.5 0.0 copy-start.1
  5.5 1.0 copy-done.1
  6.5 0.0 copy-start.2
  6.5 1.0 copy-done.2
  7.4 0.0 copy-start.3
  7.4 1.0 copy-done.3
  8.4 0.0 copy-start.4
  8.4 1.0 copy-done.4
  9.3 0.0 copy-start.5
  9.3 1.0 copy-done.5
  10.3 1.0 copy-done.6
  11.3 1.0 copy-done.7
  12.2 119.3 %shard_map.136 = (bf16[8,72,256]{2,1,0:T(8,128)(2,1)S(1)}, bf16[8,72,256]{2,1,0:T(8,128)(2,1)S(1)}, bf16[8,72,256]{2,1,0:T(8,128)(2,1)S(1)}, bf16[8,72,256]{2,1,...) custom-call(bf16[8,72,256]{2,1,0:T(8,128)(2,1)S(1)} %bitcast.84, ...), custom_call_target="tpu_custom_call" | custom-call | tf_op jit(solution)/shard_map/pallas_call | solution.py:277
  131.6 0.7 copy.24
  132.3 0.7 copy.25
  133.0 0.7 copy.26
  133.7 0.7 copy.27
  134.4 0.7 copy.28
  135.1 0.7 copy.29
  (5 shorter events, 0.0 us)
Async XLA Ops:
  0.6 4.9 %copy-start = (bf16[1,256,576]{1,2,0:T(8,128)(2,1)S(1)}, bf16[1,256,576]{1,2,0:T(8,128)(2,1)}, u32[]{:S(2)}) copy-start(bf16[1,256,576]{1,2,0:T(8,128)(2,1)} %param.9) | copy-start | bytes 884740
  5.5 1.0 copy-start.1
  6.5 1.0 copy-start.2
  7.4 1.0 copy-start.3
  8.4 1.0 copy-start.4
  9.3 1.0 copy-start.5
  10.3 1.0 copy-start.6
  11.3 1.0 copy-start.7
where the time goes:
time: 136 us
  Pallas kernels  119 us (88%)
  local copies, waits for them, and re-layouts  12.6 us (9%)
  other arithmetic  3.21 us (2%)
    pallas_call x1, Pallas kernels, shards(): pl.pallas_call(functools.partial(kernel, nz, ng), out_shape=[jax.ShapeDty...  119 us
    unnamed x22, local copies, waits for them, and re-layouts  11 us

commit v1 on v0

v1 whole, which is shorter than its diff:
```python
import functools
import math

import jax
import jax.numpy as jnp
from jax import lax
from jax.experimental import pallas as pl
from jax.experimental.pallas import tpu as pltpu
from jax.sharding import PartitionSpec as P

HEADS = 8
HDIM = 72
LANES = 128
SCALE = 1.0 / math.sqrt(HDIM)
MASKED = -1e30
MESH = pl.DeviceIdType.MESH
REACHES = ((2, 0), (4, 2), (6, 2), (8, 2))
REACH = REACHES[0][0]
BF = jnp.bfloat16
F32 = jnp.float32


def space_head(h, qs, ks, vs, cs, gq, gk, gv):
    q, k, v, c = qs[h], ks[h], vs[h], cs[h]
    first = (((0,), (0,)), ((), ()))
    last = (((1,), (1,)), ((), ()))
    plain = (((1,), (0,)), ((), ()))
    scores = lax.dot_general(k, q, first, preferred_element_type=F32) * SCALE
    peak = jnp.max(scores, axis=0, keepdims=True)
    grown = jnp.exp(scores - peak)
    weights = grown * (1.0 / jnp.sum(grown, axis=0, keepdims=True))
    low = weights.astype(BF)
    dweights = lax.dot_general(v, c, first, preferred_element_type=F32)
    dot = jnp.sum(low.astype(F32) * dweights, axis=0, keepdims=True)
    dscores = (weights * (dweights - dot)).astype(BF)
    gq[h] = (lax.dot_general(k, dscores, plain, preferred_element_type=F32) * SCALE).astype(BF)
    gk[h] = (lax.dot_general(q, dscores, last, preferred_element_type=F32) * SCALE).astype(BF)
    gv[h] = lax.dot_general(c, low, last, preferred_element_type=F32).astype(BF)


def labels_of(clip_len, label, pick, nz, ng):
    g = lax.axis_index("grp")
    shape = (nz, LANES)
    slot = lax.broadcasted_iota(jnp.int32, shape, 0)
    ids = [slot + (g - 1 + n) * nz for n in range(3)]

    def count(c, carry):
        end, found = carry
        end = end + clip_len[c]
        return end, tuple(f + jnp.where(i >= end, 1, 0) for f, i in zip(found, ids))

    zero = jnp.zeros(shape, jnp.int32)
    _, found = lax.fori_loop(0, clip_len.shape[0], count, (jnp.int32(0), (zero,) * 3))
    low, own, high = [
        jnp.where((i >= 0) & (i < nz * ng), f, -1) for f, i in zip(found, ids)
    ]
    left = own == jnp.broadcast_to(low[nz - 1 : nz], shape)
    right = own == jnp.broadcast_to(high[0:1], shape)
    label[0] = jnp.where(left, own, low).astype(F32)
    label[1] = own.astype(F32)
    label[2] = jnp.where(right, own, high).astype(F32)
    for n, flag in ((0, left), (1, right)):
        pick[n] = jnp.broadcast_to(jnp.where(flag, 1.0, 0.0)[:, None, :], (nz, 8, LANES))


def kernel(
    nz, ng,
    clip_len, qs, ks, vs, cs, qt, kt, vt, ct,
    gqs, gks, gvs, gqt, gkt, gvt,
    iqs, iks, ivs, ics,
    r1, r2, r3, o1, o2,
    fq, fk, fv, fg, fw, fl, fd, labels, pick,
    bring, in_send, in_recv, hop_send, hop_recv, out_send, out_recv, self_sem, leave,
    right_in, left_in,
):
    g = lax.axis_index("grp")
    z = lax.axis_index("seq")
    before = lax.rem(g + ng - 1, ng)
    after = lax.rem(g + 1, ng)

    def partner(d):
        return lax.rem(z + d, nz)

    def tell(sem, group, place):
        pl.semaphore_signal(sem, inc=1, device_id=(group, place), device_id_type=MESH)

    def part(ref, p):
        half = p // HEADS
        lanes = pl.ds(pl.multiple_of(half * LANES, LANES), LANES)
        return ref.at[p - half * HEADS, :, lanes]

    def send(stage, src, dst, sems_out, sems_in, d):
        return pltpu.make_async_remote_copy(
            src_ref=src, dst_ref=dst, send_sem=sems_out.at[stage, d],
            recv_sem=sems_in.at[stage, d], device_id=(g, partner(d)), device_id_type=MESH,
        )

    def bring_in(stage, ref, dst, d):
        return send(stage, part(ref, partner(d)), dst, in_send, in_recv, d)

    def keep(src, dst, i):
        return pltpu.make_async_copy(src, dst, self_sem.at[i])

    def hop(stage, ref):
        return [
            pltpu.make_async_remote_copy(
                src_ref=ref.at[1], dst_ref=ref.at[0], send_sem=hop_send.at[stage, 0],
                recv_sem=hop_recv.at[stage, 0], device_id=(after, z), device_id_type=MESH,
            ),
            pltpu.make_async_remote_copy(
                src_ref=ref.at[1], dst_ref=ref.at[2], send_sem=hop_send.at[stage, 1],
                recv_sem=hop_recv.at[stage, 1], device_id=(before, z), device_id_type=MESH,
            ),
        ]

    order = [nz // 2]
    for d in range(nz // 2 - 1, 0, -1):
        order += [d, nz - d]

    barrier = pltpu.get_barrier_semaphore()
    for d in range(REACH, 0, -1):
        tell(barrier, g, partner(d))
        tell(barrier, g, partner(nz - d))
    tell(barrier, before, z)
    tell(barrier, after, z)
    pairs = ((qs, iqs), (ks, iks), (vs, ivs), (cs, ics))
    brought = [pltpu.make_async_copy(a, b, bring.at[i]) for i, (a, b) in enumerate(pairs)]
    for c in brought:
        c.start()
    firsts = [keep(part(qt, z), r1.at[1, z, 0], 0), keep(part(kt, z), r1.at[1, z, 1], 1)]
    for c in firsts:
        c.start()
    pl.semaphore_wait(barrier, 2 * REACH + 2)

    known, rounds = 0, 0
    for limit, step in REACHES:
        if known:
            for way, far in ((right_in, nz - step), (left_in, step)):
                tell(way.at[rounds], g, partner(far))
            pl.semaphore_wait(right_in.at[rounds], 1)
            pl.semaphore_wait(left_in.at[rounds], 1)
            rounds += 1
        for k in range(known + 1, limit + 1):
            for d in (k, nz - k) if k < nz - k else (k,):
                for which, ref in ((0, qt), (1, kt)):
                    copy = bring_in(which, ref, r1.at[1, z, which], d)
                    copy.start()
                    firsts.append(copy)
        known = limit
    for c in brought:
        c.wait()

    @pl.loop(0, HEADS)
    def _(h):
        space_head(h, iqs, iks, ivs, ics, iqs, iks, ivs)

    seconds = [keep(part(ct, z), r2.at[1, z], 2)]
    seconds += [bring_in(2, ct, r2.at[1, z], d) for d in order]
    for c in seconds:
        c.start()
    leaving = [
        pltpu.make_async_copy(a, b, leave.at[i])
        for i, (a, b) in enumerate(((iqs, gqs), (iks, gks), (ivs, gvs)))
    ]
    for c in leaving:
        c.start()
    labels_of(clip_len, labels, pick, nz, ng)
    for c in firsts:
        c.wait()
    hop1 = hop(0, r1)
    for c in hop1:
        c.start()
    thirds = [keep(part(vt, z), r3.at[1, z], 3)]
    thirds += [bring_in(3, vt, r3.at[1, z], d) for d in order]
    for c in thirds:
        c.start()

    def lay(n, target, row, ref, *which):
        mine = ref[(1, row) + which].astype(F32)
        if n == 1:
            target[1, row] = mine
        else:
            other = ref[(n, row) + which].astype(F32)
            target[n, row] = jnp.where(pick[n // 2, row, 0:1, :] > 0.5, mine, other)

    def scores_of(n):
        label = labels[n]

        @pl.loop(0, nz)
        def _(i):
            s = jnp.sum(fq[n, i][None] * fk[n], axis=1) * SCALE
            same = label == labels[n, pl.ds(i, 1), :]
            s = jnp.where(same, s, MASKED)
            e = jnp.where(same, jnp.exp(s - jnp.max(s, axis=0, keepdims=True)), 0.0)
            w = e * (1.0 / jnp.sum(e, axis=0, keepdims=True))
            low = w.astype(BF).astype(F32)
            fw[n, i] = w
            fl[n, i] = jnp.broadcast_to(low[:, None, :], (nz, 8, LANES))

    def sum_over(rows, coef):
        acc = jnp.zeros((HDIM // 8, 8, LANES), F32)
        for m in range(nz):
            acc = acc + rows(m).reshape(HDIM // 8, 8, LANES) * coef(m)[None]
        return acc.reshape(HDIM, LANES)

    @pl.loop(0, nz)
    def _(i):
        lay(1, fq, i, r1, 0)
        lay(1, fk, i, r1, 1)

    scores_of(1)
    for c in hop1:
        c.wait()

    @pl.loop(0, nz)
    def _(i):
        for n in (0, 2):
            lay(n, fq, i, r1, 0)
            lay(n, fk, i, r1, 1)

    scores_of(0)
    scores_of(2)

    for c in seconds:
        c.wait()
    hop2 = hop(1, r2)
    for c in hop2:
        c.start()

    @pl.loop(0, nz)
    def _(i):
        lay(1, fg, i, r2)

    for c in hop2:
        c.wait()

    @pl.loop(0, nz)
    def _(i):
        for n in (0, 2):
            lay(n, fg, i, r2)

    def choose(j, a, b, c):
        left = pick[0, j, 0:1, :] > 0.5
        right = pick[1, j, 0:1, :] > 0.5
        return jnp.where(left, a, jnp.where(right, c, b))

    def value_grad(j):
        parts = [sum_over(lambda i: fg[n, i], lambda i: fl[n, i, j]) for n in range(3)]
        o1[j] = choose(j, *parts).astype(BF)

    def query_key_grads(i):
        parts = [sum_over(lambda j: fk[n, j], lambda j: fd[n, i, j]) for n in range(3)]
        o2[0, i] = (choose(i, *parts) * SCALE).astype(BF)
        parts = [sum_over(lambda j: fq[n, j], lambda j: fd[n, j, i]) for n in range(3)]
        o2[1, i] = (choose(i, *parts) * SCALE).astype(BF)

    def return_all(make, ways):
        def back(stage, src, dst, d):
            return send(stage, src.at[partner(d)], part(dst, z), out_send, out_recv, d)

        @pl.loop(0, nz - 1)
        def _(step):
            far = nz // 2 - (step + 1) // 2
            odd = lax.rem(step, 2)
            d = far * odd + (nz - far) * (1 - odd)
            make(partner(d))
            for stage, src, dst in ways:
                back(stage, src, dst, d).start()

        make(z)
        mine = [keep(src.at[z], part(dst, z), 4 + stage) for stage, src, dst in ways]
        for c in mine:
            c.start()
        return [back(stage, src, dst, d) for stage, src, dst in ways for d in order] + mine

    vouts = return_all(value_grad, [(0, o1, gvt)])

    for c in thirds:
        c.wait()
    hop3 = hop(2, r3)
    for c in hop3:
        c.start()

    def score_grads(n):
        @pl.loop(0, nz)
        def _(i):
            lay(n, fv, i, r3)

        @pl.loop(0, nz)
        def _(i):
            dw = jnp.sum(fg[n, i][None] * fv[n], axis=1)
            w = fw[n, i]
            low = w.astype(BF).astype(F32)
            dot = jnp.sum(low * dw, axis=0, keepdims=True)
            ds = (w * (dw - dot)).astype(BF).astype(F32)
            fd[n, i] = jnp.broadcast_to(ds[:, None, :], (nz, 8, LANES))

    score_grads(1)
    for c in hop3:
        c.wait()
    score_grads(0)
    score_grads(2)

    qkouts = return_all(query_key_grads, [(1, o2.at[0], gqt), (2, o2.at[1], gkt)])
    for c in vouts + qkouts + leaving:
        c.wait()


def hand_over(*refs):
    ins, outs, held, sems = refs[:6], refs[6:12], refs[12:18], refs[18]
    pulls = [pltpu.make_async_copy(a, b, sems.at[0, i]) for i, (a, b) in enumerate(zip(ins, held))]
    pushes = [pltpu.make_async_copy(a, b, sems.at[1, i]) for i, (a, b) in enumerate(zip(held, outs))]
    for c in pulls:
        c.start()
    for c, d in zip(pulls, pushes):
        c.wait()
        d.start()
    for c in pushes:
        c.wait()


def solution(mesh):
    nz, ng = mesh.shape["seq"], mesh.shape["grp"]

    def shards(*args):
        clip_len = args[8]
        _, tokens, channels = args[0].shape
        flat = [jnp.swapaxes(a[0], 0, 1).reshape(HEADS, HDIM, tokens) for a in args[:8]]
        anywhere = pl.BlockSpec(memory_space=pl.ANY)
        dma = pltpu.SemaphoreType.DMA
        frame = (HEADS, HDIM, tokens)
        outs = [jax.ShapeDtypeStruct(frame, BF)] * 6
        res = pl.pallas_call(
            functools.partial(kernel, nz, ng),
            out_shape=outs,
            in_specs=[pl.BlockSpec(memory_space=pltpu.SMEM)] + [anywhere] * 8,
            out_specs=[anywhere] * 6,
            scratch_shapes=[pltpu.VMEM(frame, BF)] * 4
            + [
                pltpu.VMEM((3, nz, 2, HDIM, LANES), BF),
                pltpu.VMEM((3, nz, HDIM, LANES), BF),
                pltpu.VMEM((3, nz, HDIM, LANES), BF),
                pltpu.VMEM((nz, HDIM, LANES), BF),
                pltpu.VMEM((2, nz, HDIM, LANES), BF),
                pltpu.VMEM((3, nz, HDIM, LANES), F32),
                pltpu.VMEM((3, nz, HDIM, LANES), F32),
                pltpu.VMEM((3, nz, HDIM, LANES), F32),
                pltpu.VMEM((3, nz, HDIM, LANES), F32),
                pltpu.VMEM((3, nz, nz, LANES), F32),
                pltpu.VMEM((3, nz, nz, 8, LANES), F32),
                pltpu.VMEM((3, nz, nz, 8, LANES), F32),
                pltpu.VMEM((3, nz, LANES), F32),
                pltpu.VMEM((2, nz, 8, LANES), F32),
                dma((4,)), dma((4, nz)), dma((4, nz)), dma((3, 2)), dma((3, 2)),
                dma((3, nz)), dma((3, nz)), dma((7,)), dma((3,)),
                pltpu.SemaphoreType.REGULAR((len(REACHES) - 1,)),
                pltpu.SemaphoreType.REGULAR((len(REACHES) - 1,)),
            ],
            compiler_params=pltpu.CompilerParams(
                collective_id=0, has_side_effects=True, vmem_limit_bytes=63 << 20
            ),
        )(clip_len, *flat)
        res = pl.pallas_call(
            hand_over,
            out_shape=outs,
            in_specs=[anywhere] * 6,
            out_specs=[anywhere] * 6,
            scratch_shapes=[pltpu.VMEM(frame, BF)] * 6 + [dma((2, 6))],
            compiler_params=pltpu.CompilerParams(vmem_limit_bytes=63 << 20),
        )(*res)
        return tuple(jnp.swapaxes(r.reshape(channels, tokens), 0, 1)[None] for r in res)

    cut = P(("grp", "seq"), None, None)
    return jax.shard_map(
        shards, mesh=mesh, in_specs=(cut,) * 8 + (P(),), out_specs=(cut,) * 6, check_vma=False
    )
```

time: 136 us -> 112 us (0.82)
  the two profiles are of different devices: /device:TPU:7 before, /device:TPU:1 now
where the time goes in v1:
time: 112 us
  Pallas kernels  111 us (99%)
    pallas_call x1, Pallas kernels, shards(): pl.pallas_call(functools.partial(kernel, nz, ng), out_shape=outs, in_spec...  109 us
    pallas_call x1, Pallas kernels, shards(): pl.pallas_call(hand_over, out_shape=outs, in_specs=[anywhere] * 6, out_sp...  2.27 us

profile of v1, /device:TPU:1, one launch (start us, length us, event | category | flops | bytes accessed | tf_op | source)
XLA Modules:
  0.0 111.9 jit_solution(384947908743547598)
XLA Ops:
  0.6 109.0 %shard_map.136 = (bf16[8,72,256]{2,1,0:T(8,128)(2,1)}, bf16[8,72,256]{2,1,0:T(8,128)(2,1)}, bf16[8,72,256]{2,1,0:T(8,128)(2,1)}, bf16[8,72,256]{2,1,0:T(8,128)(2...) custom-call(s32[64]{0:T(128)} %clip_len.1, bf16[8,72,256]{2,1,0:T(8,128)(2,1)} %bitcast.70, ...), custom_call_target="tpu_custom_call" | custom-call | tf_op jit(solution)/shard_map/pallas_call | solution.py:333
  109.6 2.3 %shard_map.137 = (bf16[8,72,256]{2,1,0:T(8,128)(2,1)}, bf16[8,72,256]{2,1,0:T(8,128)(2,1)}, bf16[8,72,256]{2,1,0:T(8,128)(2,1)}, bf16[8,72,256]{2,1,0:T(8,128)(2...) custom-call(bf16[8,72,256]{2,1,0:T(8,128)(2,1)} %get-tuple-element.18.refs_0_, ...), custom_call_target="tpu_custom_call" | custom-call | tf_op jit(solution)/shard_map/pallas_call | solution.py:363

commit v2 on v1

--- a/solution.py
+++ b/solution.py
@@ -212,6 +212,12 @@
     for c in hop1:
         c.wait()
 
+    for c in seconds:
+        c.wait()
+    hop2 = hop(1, r2)
+    for c in hop2:
+        c.start()
+
     @pl.loop(0, nz)
     def _(i):
         for n in (0, 2):
@@ -220,12 +226,6 @@
 
     scores_of(0)
     scores_of(2)
-
-    for c in seconds:
-        c.wait()
-    hop2 = hop(1, r2)
-    for c in hop2:
-        c.start()
 
     @pl.loop(0, nz)
     def _(i):
@@ -247,12 +247,6 @@
     def value_grad(j):
         parts = [sum_over(lambda i: fg[n, i], lambda i: fl[n, i, j]) for n in range(3)]
         o1[j] = choose(j, *parts).astype(BF)
-
-    def query_key_grads(i):
-        parts = [sum_over(lambda j: fk[n, j], lambda j: fd[n, i, j]) for n in range(3)]
-        o2[0, i] = (choose(i, *parts) * SCALE).astype(BF)
-        parts = [sum_over(lambda j: fq[n, j], lambda j: fd[n, j, i]) for n in range(3)]
-        o2[1, i] = (choose(i, *parts) * SCALE).astype(BF)
 
     def return_all(make, ways):
         def back(stage, src, dst, d):
@@ -281,27 +275,42 @@
     for c in hop3:
         c.start()
 
-    def score_grads(n):
+    def lay_values(*sets):
         @pl.loop(0, nz)
         def _(i):
-            lay(n, fv, i, r3)
-
-        @pl.loop(0, nz)
-        def _(i):
-            dw = jnp.sum(fg[n, i][None] * fv[n], axis=1)
-            w = fw[n, i]
-            low = w.astype(BF).astype(F32)
-            dot = jnp.sum(low * dw, axis=0, keepdims=True)
-            ds = (w * (dw - dot)).astype(BF).astype(F32)
-            fd[n, i] = jnp.broadcast_to(ds[:, None, :], (nz, 8, LANES))
-
-    score_grads(1)
+            for n in sets:
+                lay(n, fv, i, r3)
+
+    def score_grad_row(n, i):
+        dw = jnp.sum(fg[n, i][None] * fv[n], axis=1)
+        w = fw[n, i]
+        low = w.astype(BF).astype(F32)
+        dot = jnp.sum(low * dw, axis=0, keepdims=True)
+        ds = (w * (dw - dot)).astype(BF).astype(F32)
+        fd[n, i] = jnp.broadcast_to(ds[:, None, :], (nz, 8, LANES))
+
+    lay_values(1)
+
+    @pl.loop(0, nz)
+    def _(i):
+        score_grad_row(1, i)
+
     for c in hop3:
         c.wait()
-    score_grads(0)
-    score_grads(2)
-
-    qkouts = return_all(query_key_grads, [(1, o2.at[0], gqt), (2, o2.at[1], gkt)])
+    lay_values(0, 2)
+
+    def query_grad(i):
+        score_grad_row(0, i)
+        score_grad_row(2, i)
+        parts = [sum_over(lambda j: fk[n, j], lambda j: fd[n, i, j]) for n in range(3)]
+        o2[0, i] = (choose(i, *parts) * SCALE).astype(BF)
+
+    def key_grad(j):
+        parts = [sum_over(lambda i: fq[n, i], lambda i: fd[n, i, j]) for n in range(3)]
+        o2[1, j] = (choose(j, *parts) * SCALE).astype(BF)
+
+    qkouts = return_all(query_grad, [(1, o2.at[0], gqt)])
+    qkouts += return_all(key_grad, [(2, o2.at[1], gkt)])
     for c in vouts + qkouts + leaving:
         c.wait()
 

time: 112 us -> 109 us (0.973)
  the two profiles are of different devices: /device:TPU:1 before, /device:TPU:7 now
where the time goes in v2:
time: 109 us; the launch traced here: 107 us
  Pallas kernels  107 us (98%)
    pallas_call x1, Pallas kernels, shards(): pl.pallas_call(functools.partial(kernel, nz, ng), out_shape=outs, in_spec...  104 us
    pallas_call x1, Pallas kernels, shards(): pl.pallas_call(hand_over, out_shape=outs, in_specs=[anywhere] * 6, out_sp...  2.27 us

profile of v2, /device:TPU:7, one launch (start us, length us, event | category | flops | bytes accessed | tf_op | source)
XLA Modules:
  0.0 107.2 jit_solution(672287623691983458)
XLA Ops:
  0.6 104.3 %shard_map.136 = (bf16[8,72,256]{2,1,0:T(8,128)(2,1)}, bf16[8,72,256]{2,1,0:T(8,128)(2,1)}, bf16[8,72,256]{2,1,0:T(8,128)(2,1)}, bf16[8,72,256]{2,1,0:T(8,128)(2...) custom-call(s32[64]{0:T(128)} %clip_len.1, bf16[8,72,256]{2,1,0:T(8,128)(2,1)} %bitcast.70, ...), custom_call_target="tpu_custom_call" | custom-call | tf_op jit(solution)/shard_map/pallas_call | solution.py:342
  104.9 2.3 %shard_map.137 = (bf16[8,72,256]{2,1,0:T(8,128)(2,1)}, bf16[8,72,256]{2,1,0:T(8,128)(2,1)}, bf16[8,72,256]{2,1,0:T(8,128)(2,1)}, bf16[8,72,256]{2,1,0:T(8,128)(2...) custom-call(bf16[8,72,256]{2,1,0:T(8,128)(2,1)} %get-tuple-element.18.refs_0_, ...), custom_call_target="tpu_custom_call" | custom-call | tf_op jit(solution)/shard_map/pallas_call | solution.py:372

commit v3 on v2

--- a/solution.py
+++ b/solution.py
@@ -65,13 +65,13 @@
 
 def kernel(
     nz, ng,
-    clip_len, qs, ks, vs, cs, qt, kt, vt, ct,
+    clip_src, qs, ks, vs, cs, qt, kt, vt, ct,
     gqs, gks, gvs, gqt, gkt, gvt,
     iqs, iks, ivs, ics,
     r1, r2, r3, o1, o2,
     fq, fk, fv, fg, fw, fl, fd, labels, pick,
     bring, in_send, in_recv, hop_send, hop_recv, out_send, out_recv, self_sem, leave,
-    right_in, left_in,
+    right_in, left_in, clip_len,
 ):
     g = lax.axis_index("grp")
     z = lax.axis_index("seq")
@@ -123,7 +123,7 @@
         tell(barrier, g, partner(nz - d))
     tell(barrier, before, z)
     tell(barrier, after, z)
-    pairs = ((qs, iqs), (ks, iks), (vs, ivs), (cs, ics))
+    pairs = ((qs, iqs), (ks, iks), (vs, ivs), (cs, ics), (clip_src, clip_len))
     brought = [pltpu.make_async_copy(a, b, bring.at[i]) for i, (a, b) in enumerate(pairs)]
     for c in brought:
         c.start()
@@ -342,7 +342,7 @@
         res = pl.pallas_call(
             functools.partial(kernel, nz, ng),
             out_shape=outs,
-            in_specs=[pl.BlockSpec(memory_space=pltpu.SMEM)] + [anywhere] * 8,
+            in_specs=[anywhere] * 9,
             out_specs=[anywhere] * 6,
             scratch_shapes=[pltpu.VMEM(frame, BF)] * 4
             + [
@@ -360,10 +360,11 @@
                 pltpu.VMEM((3, nz, nz, 8, LANES), F32),
                 pltpu.VMEM((3, nz, LANES), F32),
                 pltpu.VMEM((2, nz, 8, LANES), F32),
-                dma((4,)), dma((4, nz)), dma((4, nz)), dma((3, 2)), dma((3, 2)),
+                dma((5,)), dma((4, nz)), dma((4, nz)), dma((3, 2)), dma((3, 2)),
                 dma((3, nz)), dma((3, nz)), dma((7,)), dma((3,)),
                 pltpu.SemaphoreType.REGULAR((len(REACHES) - 1,)),
                 pltpu.SemaphoreType.REGULAR((len(REACHES) - 1,)),
+                pltpu.SMEM(clip_len.shape, clip_len.dtype),
             ],
             compiler_params=pltpu.CompilerParams(
                 collective_id=0, has_side_effects=True, vmem_limit_bytes=63 << 20

time: 109 us -> 109 us (level)
  no operation moved by 1% of the time
where the time goes in v3:
time: 109 us; the launch traced here: 107 us
  Pallas kernels  106 us (97%)
    pallas_call x1, Pallas kernels, shards(): pl.pallas_call(functools.partial(kernel, nz, ng), out_shape=outs, in_spec...  104 us
    pallas_call x1, Pallas kernels, shards(): pl.pallas_call(hand_over, out_shape=outs, in_specs=[anywhere] * 6, out_sp...  2.27 us

profile of v3, /device:TPU:7, one launch (start us, length us, event | category | flops | bytes accessed | tf_op | source)
XLA Modules:
  0.0 106.5 jit_solution(11575066404519876435)
XLA Ops:
  0.6 103.6 %shard_map.136 = (bf16[8,72,256]{2,1,0:T(8,128)(2,1)}, bf16[8,72,256]{2,1,0:T(8,128)(2,1)}, bf16[8,72,256]{2,1,0:T(8,128)(2,1)}, bf16[8,72,256]{2,1,0:T(8,128)(2...) custom-call(s32[64]{0:T(128)} %clip_src.1, bf16[8,72,256]{2,1,0:T(8,128)(2,1)} %bitcast.70, ...), custom_call_target="tpu_custom_call" | custom-call | tf_op jit(solution)/shard_map/pallas_call | solution.py:342
  104.3 2.3 %shard_map.137 = (bf16[8,72,256]{2,1,0:T(8,128)(2,1)}, bf16[8,72,256]{2,1,0:T(8,128)(2,1)}, bf16[8,72,256]{2,1,0:T(8,128)(2,1)}, bf16[8,72,256]{2,1,0:T(8,128)(2...) custom-call(bf16[8,72,256]{2,1,0:T(8,128)(2,1)} %get-tuple-element.18.refs_0_, ...), custom_call_target="tpu_custom_call" | custom-call | tf_op jit(solution)/shard_map/pallas_call | solution.py:373

commit v4 on v3

--- a/solution.py
+++ b/solution.py
@@ -125,14 +125,11 @@
     tell(barrier, after, z)
     pairs = ((qs, iqs), (ks, iks), (vs, ivs), (cs, ics), (clip_src, clip_len))
     brought = [pltpu.make_async_copy(a, b, bring.at[i]) for i, (a, b) in enumerate(pairs)]
-    for c in brought:
-        c.start()
-    firsts = [keep(part(qt, z), r1.at[1, z, 0], 0), keep(part(kt, z), r1.at[1, z, 1], 1)]
-    for c in firsts:
-        c.start()
+    own_first = [keep(part(qt, z), r1.at[1, z, 0], 0), keep(part(kt, z), r1.at[1, z, 1], 1)]
     pl.semaphore_wait(barrier, 2 * REACH + 2)
 
     known, rounds = 0, 0
+    firsts = list(own_first)
     for limit, step in REACHES:
         if known:
             for way, far in ((right_in, nz - step), (left_in, step)):
@@ -140,12 +137,15 @@
             pl.semaphore_wait(right_in.at[rounds], 1)
             pl.semaphore_wait(left_in.at[rounds], 1)
             rounds += 1
-        for k in range(known + 1, limit + 1):
+        for k in range(limit, known, -1):
             for d in (k, nz - k) if k < nz - k else (k,):
                 for which, ref in ((0, qt), (1, kt)):
                     copy = bring_in(which, ref, r1.at[1, z, which], d)
                     copy.start()
                     firsts.append(copy)
+        if not known:
+            for c in brought + own_first:
+                c.start()
         known = limit
     for c in brought:
         c.wait()

time: 109 us -> 109 us (level)
  no operation moved by 1% of the time
where the time goes in v4:
time: 109 us; the launch traced here: 107 us
  Pallas kernels  106 us (97%)
    pallas_call x1, Pallas kernels, shards(): pl.pallas_call(functools.partial(kernel, nz, ng), out_shape=outs, in_spec...  104 us
    pallas_call x1, Pallas kernels, shards(): pl.pallas_call(hand_over, out_shape=outs, in_specs=[anywhere] * 6, out_sp...  2.27 us

profile of v4, /device:TPU:7, one launch (start us, length us, event | category | flops | bytes accessed | tf_op | source)
XLA Modules:
  0.0 107.1 jit_solution(18108103248718210388)
XLA Ops:
  0.6 104.2 %shard_map.136 = (bf16[8,72,256]{2,1,0:T(8,128)(2,1)}, bf16[8,72,256]{2,1,0:T(8,128)(2,1)}, bf16[8,72,256]{2,1,0:T(8,128)(2,1)}, bf16[8,72,256]{2,1,0:T(8,128)(2...) custom-call(s32[64]{0:T(128)} %clip_src.1, bf16[8,72,256]{2,1,0:T(8,128)(2,1)} %bitcast.70, ...), custom_call_target="tpu_custom_call" | custom-call | tf_op jit(solution)/shard_map/pallas_call | solution.py:342
  104.8 2.3 %shard_map.137 = (bf16[8,72,256]{2,1,0:T(8,128)(2,1)}, bf16[8,72,256]{2,1,0:T(8,128)(2,1)}, bf16[8,72,256]{2,1,0:T(8,128)(2,1)}, bf16[8,72,256]{2,1,0:T(8,128)(2...) custom-call(bf16[8,72,256]{2,1,0:T(8,128)(2,1)} %get-tuple-element.18.refs_0_, ...), custom_call_target="tpu_custom_call" | custom-call | tf_op jit(solution)/shard_map/pallas_call | solution.py:373

commit v5 on v4

--- a/solution.py
+++ b/solution.py
@@ -147,6 +147,10 @@
             for c in brought + own_first:
                 c.start()
         known = limit
+    seconds = [keep(part(ct, z), r2.at[1, z], 2)]
+    seconds += [bring_in(2, ct, r2.at[1, z], d) for d in order]
+    for c in seconds:
+        c.start()
     for c in brought:
         c.wait()
 
@@ -154,10 +158,6 @@
     def _(h):
         space_head(h, iqs, iks, ivs, ics, iqs, iks, ivs)
 
-    seconds = [keep(part(ct, z), r2.at[1, z], 2)]
-    seconds += [bring_in(2, ct, r2.at[1, z], d) for d in order]
-    for c in seconds:
-        c.start()
     leaving = [
         pltpu.make_async_copy(a, b, leave.at[i])
         for i, (a, b) in enumerate(((iqs, gqs), (iks, gks), (ivs, gvs)))

time: 109 us -> 109 us (level)
  no operation moved by 1% of the time
where the time goes in v5:
time: 109 us; the launch traced here: 107 us
  Pallas kernels  106 us (97%)
    pallas_call x1, Pallas kernels, shards(): pl.pallas_call(functools.partial(kernel, nz, ng), out_shape=outs, in_spec...  104 us
    pallas_call x1, Pallas kernels, shards(): pl.pallas_call(hand_over, out_shape=outs, in_specs=[anywhere] * 6, out_sp...  2.27 us

profile of v5, /device:TPU:7, one launch (start us, length us, event | category | flops | bytes accessed | tf_op | source)
XLA Modules:
  0.0 107.1 jit_solution(4200199915513953063)
XLA Ops:
  0.6 104.2 %shard_map.136 = (bf16[8,72,256]{2,1,0:T(8,128)(2,1)}, bf16[8,72,256]{2,1,0:T(8,128)(2,1)}, bf16[8,72,256]{2,1,0:T(8,128)(2,1)}, bf16[8,72,256]{2,1,0:T(8,128)(2...) custom-call(s32[64]{0:T(128)} %clip_src.1, bf16[8,72,256]{2,1,0:T(8,128)(2,1)} %bitcast.70, ...), custom_call_target="tpu_custom_call" | custom-call | tf_op jit(solution)/shard_map/pallas_call | solution.py:342
  104.8 2.3 %shard_map.137 = (bf16[8,72,256]{2,1,0:T(8,128)(2,1)}, bf16[8,72,256]{2,1,0:T(8,128)(2,1)}, bf16[8,72,256]{2,1,0:T(8,128)(2,1)}, bf16[8,72,256]{2,1,0:T(8,128)(2...) custom-call(bf16[8,72,256]{2,1,0:T(8,128)(2,1)} %get-tuple-element.18.refs_0_, ...), custom_call_target="tpu_custom_call" | custom-call | tf_op jit(solution)/shard_map/pallas_call | solution.py:373
